TPU v7x, 128 devices: a whole 4x4x4 slice. The times are simulated.
128 devices in a mesh: row: 8 (over x_lo, y), col: 16 (over x_hi, z, core).
Axes of the slice: x: 4 (x_hi: 2, x_lo: 2; x = x_hi * 2 + x_lo), y: 4, z: 4, core: 2. Of those that a mesh axis runs over, the one named last changes fastest.
Arguments:
- traces: bfloat16 [384, 60, 8192], P(('row', 'col')), may hold values from -80 to 80
- masks: int32 [384, 60], P(('row', 'col')), may hold values from 0 to 1, as said below
Outputs:
- correlations: float32 [384, 384, 2048], P('row', 'col')
Inputs may be any that keep to these rules, and one draw needn't show every extreme that they name: `masks`: 1 marks a usable trace of a channel, 0 one left out of the stack; a channel may be flagged 0 in every trace.
All inputs are finite; a program needn't handle non-finite values.
Results may differ from a plain program's by a relative error of at most 0.0052.
Values may be sent and summed in bfloat16 or wider, within the bound.
No kernel may reach another device: no remote copies, remote signals or barrier semaphores. Data moves between devices by JAX's collectives and lax.ppermute only.
A program may use at most 320 MiB of HBM per device.

v0:
```python
import math

import jax
import jax.numpy as jnp
from jax import lax
from jax.sharding import PartitionSpec as P

TRACES = 60
SAMPLES = 8192
BINS = 1024
LOW_BIN = 33
LAGS = 2048
SMOOTH = 64
EDGE = 64


def from_root(block, axis, source):
    block = jnp.where(lax.axis_index(axis) == source, block, jnp.zeros_like(block))
    return lax.psum(block, axis)


def dft_table():
    samples_at = jnp.arange(SAMPLES, dtype=jnp.int32)[:, None]
    passband = (LOW_BIN + jnp.arange(BINS, dtype=jnp.int32))[None, :]
    phases = samples_at * passband % SAMPLES
    angles = phases.astype(jnp.float32) * (2.0 * math.pi / SAMPLES)
    return jnp.concatenate([jnp.cos(angles), -jnp.sin(angles)], axis=1).astype(jnp.bfloat16)


def lag_table():
    passband = (LOW_BIN + jnp.arange(BINS, dtype=jnp.int32))[:, None]
    shifts = (jnp.arange(LAGS, dtype=jnp.int32) - LAGS // 2 + SAMPLES)[None, :]
    phases = passband * shifts % SAMPLES
    angles = phases.astype(jnp.float32) * (2.0 * math.pi / SAMPLES)
    factor = 2.0 / math.sqrt(BINS)
    return (factor * jnp.concatenate([jnp.cos(angles), -jnp.sin(angles)], axis=0)).astype(
        jnp.bfloat16
    )


def band_taper():
    position = jnp.arange(BINS, dtype=jnp.int32)
    distance = jnp.minimum(position, BINS - 1 - position).astype(jnp.float32)
    ramp_level = jnp.minimum((distance + 0.5) / EDGE, 1.0)
    return 0.5 - 0.5 * jnp.cos(math.pi * ramp_level)


def smoother():
    position = jnp.arange(BINS, dtype=jnp.int32)
    nearby = (jnp.abs(position[:, None] - position[None, :]) <= SMOOTH).astype(jnp.float32)
    return nearby / jnp.sum(nearby, axis=0, keepdims=True)


def whiten(spectrum):
    real_part = spectrum[:, :BINS]
    imag_part = spectrum[:, BINS:]
    magnitude = jnp.sqrt(real_part * real_part + imag_part * imag_part)
    smoothed = jnp.dot(magnitude, smoother(), precision=lax.Precision.HIGHEST) + 1e-06
    weights = band_taper()[None, :] / smoothed
    return jnp.concatenate([real_part * weights, imag_part * weights], axis=1)


def local(traces, masks):
    own_rows = traces.shape[0]
    flat_rows = traces.reshape(own_rows * TRACES, SAMPLES)
    spectrum = jnp.dot(flat_rows, dft_table(), preferred_element_type=jnp.float32)
    whitened = whiten(spectrum).reshape(own_rows, TRACES, 2 * BINS)
    usable = masks.astype(jnp.float32)
    spectra = (whitened * usable[:, :, None]).astype(jnp.bfloat16)
    usable_wire = masks.astype(jnp.bfloat16)
    rows_axis = lax.axis_size("row")
    cols_axis = lax.axis_size("col")
    channels = own_rows * rows_axis * cols_axis
    row_block = channels // rows_axis
    col_block = channels // cols_axis
    factor = cols_axis // rows_axis
    col_place = lax.axis_index("col")
    row_spec = lax.all_gather(spectra, "col", axis=0, tiled=True)
    row_mask = lax.all_gather(usable_wire, "col", axis=0, tiled=True)
    offset = col_place % factor * col_block
    local_spec = lax.dynamic_slice_in_dim(row_spec, offset, col_block, 0)
    local_mask = lax.dynamic_slice_in_dim(row_mask, offset, col_block, 0)
    col_spec = from_root(local_spec, "row", col_place // factor)
    col_mask = from_root(local_mask, "row", col_place // factor)
    left_real = jnp.concatenate([row_spec[:, :, :BINS], row_spec[:, :, BINS:]], axis=1)
    left_imag = jnp.concatenate([row_spec[:, :, BINS:], -row_spec[:, :, :BINS]], axis=1)
    right_both = jnp.concatenate([col_spec[:, :, :BINS], col_spec[:, :, BINS:]], axis=1)
    cross_real = jnp.einsum(
        "atf,btf->abf", left_real, right_both, preferred_element_type=jnp.float32
    )
    cross_imag = jnp.einsum(
        "atf,btf->abf", left_imag, right_both, preferred_element_type=jnp.float32
    )
    summed = jnp.concatenate([cross_real, cross_imag], axis=2)
    tallies = jnp.dot(row_mask, col_mask.T, preferred_element_type=jnp.float32)
    stacked = (summed / jnp.maximum(tallies, 1.0)[:, :, None]).astype(jnp.bfloat16)
    result = jnp.dot(
        stacked.reshape(row_block * col_block, 2 * BINS),
        lag_table(),
        preferred_element_type=jnp.float32,
    )
    return result.reshape(row_block, col_block, LAGS)


def solution(mesh):
    in_specs = (P(("row", "col"), None, None), P(("row", "col"), None))
    out_specs = P("row", "col", None)
    return jax.shard_map(local, mesh=mesh, in_specs=in_specs, out_specs=out_specs, check_vma=False)
```

profile of v0, /device:TPU:1, one launch (start us, length us, event | category | flops | bytes accessed | tf_op | source)
XLA Modules:
  0.0 648.4 jit_solution(17958419968451002791)
XLA Ops:
  6.5 0.2 convert_reduce_fusion
  6.8 136.2 %cosine_convert_fusion = (bf16[8192,1024]{1,0:T(8,128)(2,1)}, bf16[8192,1024]{1,0:T(8,128)(2,1)}) fusion(s32[1024]{0:T(1024)S(1)} %iota_add_fusion.1), kind=kLoop, calls=%fused_computation.11 | loop fusion | flops 142606336 | bytes 33558528 | tf_op jit(solution)/shard_map/convert
  143.0 2.1 reshape.51
  145.1 14.2 %fusion.36 = f32[180,2048]{1,0:T(8,128)S(1)} fusion(bf16[180,8192]{1,0:T(8,128)(2,1)} %reshape.51, bf16[8192,1024]{1,0:T(8,128)(2,1)} %get-tuple-element.14, bf16[8192,1024]{1,0:T(8,128)(2,1)} %get-tuple-element.13), kind=kOutput, calls=%fused_computation.48 | convolution fusion | flops 6106906624 | bytes 37978112 | tf_op jit(solution)/shard_map/dot_general | solution.py:66
  159.3 2.9 slice_multiply_fusion.1
  162.3 0.1 pad_maximum_fusion.1
  162.4 0.1 reshape.52
  162.5 1.0 multiply_convert_fusion
  163.6 0.0 all-gather.3.cloned.1.call-update
  163.6 0.2 all-reduce.2.cloned.1.call-start
  163.8 94.4 %all-gather.3.cloned.1.call-done = bf16[48,60,2048]{2,1,0:T(8,128)(2,1)} async-done(((bf16[3,60,2048]{2,1,0:T(8,128)(2,1)}), bf16[48,60,2048]{2,1,0:T(8,128)(2,1)}) %all-gather.3.cloned.1.call-update) | async-done | bytes 11796496 | tf_op jit(solution)/shard_map/all_gather | solution.py:78
  258.3 6.6 %constant_dynamic-slice_fusion = bf16[24,60,2048]{2,1,0:T(8,128)(2,1)} fusion(bf16[48,60,2048]{2,1,0:T(8,128)(2,1)} %all-gather.3.cloned.1.call-done, s32[]{:T(128)S(6)} %select_n.52), kind=kLoop, calls=%fused_computation.78 | loop fusion | bytes 11796484 | tf_op jit(solution)/shard_map/dynamic_slice | solution.py:81
  264.9 14.4 %copy.19 = bf16[24,60,2048]{1,0,2:T(8,128)(2,1)} copy(bf16[24,60,2048]{2,1,0:T(8,128)(2,1)} %constant_dynamic-slice_fusion) | data formatting | bytes 11796480
  279.3 10.6 %broadcast_select_fusion = bf16[24,60,2048]{1,0,2:T(8,128)(2,1)} fusion(bf16[24,60,2048]{1,0,2:T(8,128)(2,1)} %copy.19, pred[]{:T(512)S(6)} %eq.10), kind=kLoop, calls=%fused_computation.30 | loop fusion | flops 2949120 | bytes 11796481 | tf_op jit(solution)/shard_map/jit(_where)/select_n | solution.py:18
  289.9 0.0 all-reduce.2.cloned.1.call-update
  290.0 19.3 %all-gather = bf16[16,3,60]{2,1,0:T(4,128)(2,1)S(1)} all-gather(bf16[1,3,60]{2,1,0:T(4,128)(2,1)S(1)} %get-tuple-element.15), channel_id=1, replica_groups=mesh['row'=8,'col'=16] {'col'}, dimensions={0}, use_global_device_ids=true | all-gather | bytes 6120 | tf_op jit(solution)/shard_map/all_gather | solution.py:79
  309.3 19.5 %psum.15 = bf16[24,60]{1,0:T(8,128)(2,1)S(1)} all-reduce(bf16[24,60]{1,0:T(8,128)(2,1)S(1)} %dynamic-slice_select_fusion), channel_id=1, replica_groups=mesh['row'=8,'col'=16] {'row'}, use_global_device_ids=true, to_apply=%region_2.3 | all-reduce | flops 1440 | bytes 5760 | tf_op jit(solution)/shard_map/psum | solution.py:19
  328.8 0.1 fusion.42
  328.9 0.1 copy.18
  329.0 35.4 %fusion.34 = (f32[1024,2048]{1,0:T(8,128)}, f32[1024,2048]{1,0:T(8,128)}) fusion(s32[2048]{0:T(1024)S(1)} %iota_add_fusion, s32[1024]{0:T(1024)S(1)} %iota_add_fusion.1), kind=kLoop, calls=%fused_computation.45 | loop fusion | flops 31457280 | bytes 16789504 | tf_op jit(solution)/shard_map/cos | solution.py:36
  364.4 11.1 %fusion.65 = (bf16[48,60,1024]{2,1,0:T(8,128)(2,1)}, bf16[48,60,1024]{2,1,0:T(8,128)(2,1)}) fusion(bf16[48,60,2048]{2,1,0:T(8,128)(2,1)} %all-gather.3.cloned.1.call-done), kind=kLoop, calls=%fused_computation.86 | loop fusion | bytes 23592960 | tf_op jit(solution)/shard_map/slice | solution.py:85
  375.5 15.9 %copy.20 = bf16[48,60,1024]{1,0,2:T(8,128)(2,1)} copy(bf16[48,60,1024]{2,1,0:T(8,128)(2,1)} %get-tuple-element.8) | data formatting | bytes 11796480
  391.4 16.0 %copy.21 = bf16[48,60,1024]{1,0,2:T(8,128)(2,1)} copy(bf16[48,60,1024]{2,1,0:T(8,128)(2,1)} %get-tuple-element.7) | data formatting | bytes 11796480
  407.4 11.4 %neg.10 = bf16[48,60,1024]{1,0,2:T(8,128)(2,1)} negate(bf16[48,60,1024]{1,0,2:T(8,128)(2,1)} %copy.20) | non-fusion elementwise | flops 2949120 | bytes 11796480 | tf_op jit(solution)/shard_map/neg | solution.py:86
  418.8 132.3 %all-reduce.2.cloned.1.call-done = bf16[24,60,2048]{1,0,2:T(8,128)(2,1)} async-done(((bf16[24,60,2048]{1,0,2:T(8,128)(2,1)}), bf16[24,60,2048]{1,0,2:T(8,128)(2,1)}) %all-reduce.2.cloned.1.call-update) | async-done | bytes 5898256 | tf_op jit(solution)/shard_map/psum | solution.py:19
  551.2 8.4 %fusion.64 = (bf16[24,60,1024]{1,0,2:T(8,128)(2,1)S(1)}, bf16[24,60,1024]{1,0,2:T(8,128)(2,1)}) fusion(bf16[24,60,2048]{1,0,2:T(8,128)(2,1)} %all-reduce.2.cloned.1.call-done), kind=kLoop, calls=%fused_computation.85 | loop fusion | bytes 11796480 | tf_op jit(solution)/shard_map/slice | solution.py:87
  559.5 2.6 copy-done
  562.1 19.7 %fusion.31 = f32[48,24,1024]{0,1,2:T(8,128)} fusion(bf16[48,60,1024]{1,0,2:T(8,128)(2,1)} %copy.21, bf16[48,60,1024]{1,0,2:T(8,128)(2,1)} %copy.20, bf16[24,60,1024]{1,0,2:T(8,128)(2,1)} %get-tuple-element.6, bf16[24,60,1024]{1,0,2:T(8,128)(2,1)S(1)} %get-tuple-element.5), kind=kOutput, calls=%fused_computation.44 | convolution fusion | flops 318504960 | bytes 22413312 | tf_op jit(solution)/shard_map/atf,btf->abf/dot_general | solution.py:88
  581.8 10.0 %copy.16 = f32[48,24,1024]{2,1,0:T(8,128)} copy(f32[48,24,1024]{0,1,2:T(8,128)} %fusion.31) | data formatting | bytes 9437184 | tf_op jit(solution)/shard_map/atf,btf->abf/transpose | solution.py:88
  591.8 21.0 %fusion.28 = f32[48,24,1024]{0,1,2:T(8,128)} fusion(bf16[48,60,1024]{1,0,2:T(8,128)(2,1)} %neg.10, bf16[48,60,1024]{1,0,2:T(8,128)(2,1)} %copy.21, bf16[24,60,1024]{1,0,2:T(8,128)(2,1)} %get-tuple-element.6, bf16[24,60,1024]{1,0,2:T(8,128)(2,1)} %copy-done), kind=kOutput, calls=%fused_computation.43 | convolution fusion | flops 318504960 | bytes 22413312 | tf_op jit(solution)/shard_map/atf,btf->abf/dot_general | solution.py:91
  612.8 10.0 %copy.17 = f32[48,24,1024]{2,1,0:T(8,128)} copy(f32[48,24,1024]{0,1,2:T(8,128)} %fusion.28) | data formatting | bytes 9437184 | tf_op jit(solution)/shard_map/atf,btf->abf/transpose | solution.py:91
  622.8 18.8 %fusion.24 = f32[48,24,2048]{2,1,0:T(8,128)} fusion(f32[1024,2048]{1,0:T(8,128)} %get-tuple-element.12, f32[1024,2048]{1,0:T(8,128)} %get-tuple-element.11, f32[48,24,1024]{2,1,0:T(8,128)} %copy.17, f32[48,24,1024]{2,1,0:T(8,128)} %copy.16, f32[48,24]{1,0:T(8,128)S(1)} %copy.18), kind=kOutput, calls=%fused_computation.37 | convolution fusion | flops 9683337216 | bytes 35656192 | tf_op jit(solution)/shard_map/dot_general | solution.py:97
  (12 shorter events, 0.1 us)
Async XLA Ops:
  6.5 251.7 %all-gather.3.cloned.1.call-start = ((), (), s32[]{:S(2)}) async-start(), calls=%async_computation | async-start | bytes 13369344 | tf_op jit(solution)/shard_map/all_gather | solution.py:78
  6.8 136.2 %copy-start.1 = (bf16[3,60,8192]{2,1,0:T(8,128)(2,1)S(1)}, bf16[3,60,8192]{2,1,0:T(8,128)(2,1)}, u32[]{:S(2)}) copy-start(bf16[3,60,8192]{2,1,0:T(8,128)(2,1)} %param.2) | copy-start | bytes 8847364
  159.3 3.2 copy-start.2
  163.6 387.6 %all-reduce.2.cloned.1.call-start = ((), (), s32[]{:S(2)}) async-start(), calls=%async_computation.1 | async-start | bytes 25165824 | tf_op jit(solution)/shard_map/psum | solution.py:19
  559.5 2.6 copy-start
Sparse Core Ops, SparseCore 0:
  163.7 94.5 all-gather.2
  290.1 261.0 all-reduce.1
where the time goes:
time: 650 us; the launch traced here: 648 us
  waiting for transfers between devices  227 us (35%)
  other arithmetic  195 us (30%)
  local copies, waits for them, and re-layouts  97.3 us (15%)
  matrix products  76.7 us (12%)
  blocking collectives  38.8 us (6%)
  between operations  13.5 us (2%)
    another operation x1, other arithmetic  136 us
    psum x1, waiting for transfers between devices, from_root(): return lax.psum(block, axis)  132 us
    all_gather x1, waiting for transfers between devices, local(): row_spec = lax.all_gather(spectra, 'col', axis=0, tiled=True)  94.4 us
    unnamed x10, local copies, waits for them, and re-layouts  48.9 us
    cos x1, other arithmetic, lag_table(): jnp.cos(angles)  35.4 us
    dot_general x1, matrix products, local(): jnp.einsum('atf,btf->abf', left_imag, right_both, preferred_element_type=...  21 us
    dot_general x1, matrix products, local(): jnp.einsum('atf,btf->abf', left_real, right_both, preferred_element_type=...  19.7 us
    psum x1, blocking collectives, from_root(): return lax.psum(block, axis)  19.5 us
  transfers between devices with their start and end apart: 2, of which 2 were waited for; matrix products, arithmetic and copies ran while one was open for 14% of the time, Pallas kernels for 0%

commit v1 on v0

v1 whole, which is shorter than its diff:
```python
import math

import jax
import jax.numpy as jnp
import ml_dtypes
import numpy as np
from jax import lax
from jax.experimental import pallas as pl
from jax.experimental.pallas import tpu as pltpu
from jax.sharding import PartitionSpec as P

TRACES = 60
SAMPLES = 8192
BINS = 1024
LOW_BIN = 33
LAGS = 2048
SMOOTH = 64
EDGE = 64

F32 = jnp.float32
BF16 = jnp.bfloat16
MIB = 1 << 20

OWN = 3
SLOT = 64
QUARTER = SAMPLES // 4
CLASS = BINS // 4
PER = 8
DEVICES = BINS // PER
ROWS = 8
COLS = 16
CHANNELS = OWN * DEVICES
NT = (((1,), (1,)), ((), ()))


def bin_order():
    k = np.arange(BINS)
    return np.concatenate([k[(k + LOW_BIN) % 4 == q] for q in range(4)])


def angles_of(phases):
    return (phases % SAMPLES).astype(np.float32) * np.float32(2.0 * math.pi / SAMPLES)


def cosine(angles):
    return np.cos(angles.astype(np.float64)).astype(np.float32)


def sine(angles):
    return np.sin(angles.astype(np.float64)).astype(np.float32)


def forward_tables():
    bins = (LOW_BIN + bin_order()).reshape(4, 1, CLASS)
    angles = angles_of(np.arange(QUARTER).reshape(1, QUARTER, 1) * bins)
    return np.concatenate([cosine(angles), -sine(angles)], axis=2).astype(ml_dtypes.bfloat16)


def lag_table():
    bins = (LOW_BIN + bin_order()).reshape(DEVICES, PER, 1)
    angles = angles_of(bins * (np.arange(LAGS) - LAGS // 2 + SAMPLES).reshape(1, 1, LAGS))
    both = np.stack([cosine(angles), -sine(angles)], axis=1) * np.float32(2.0 / math.sqrt(BINS))
    return both.reshape(2 * BINS, LAGS).astype(ml_dtypes.bfloat16)


def window_tables():
    order = bin_order()
    nearby = np.abs(order[:, None] - order[None, :]) <= SMOOTH
    distance = np.minimum(order, BINS - 1 - order).astype(np.float32)
    ramp = np.minimum((distance + np.float32(0.5)) / np.float32(EDGE), np.float32(1.0))
    taper = np.float32(0.5) - np.float32(0.5) * cosine(np.float32(math.pi) * ramp)
    rows = np.zeros((8, BINS), np.float32)
    rows[0] = taper
    rows[1] = np.float32(1.0) / nearby.sum(axis=0).astype(np.float32)
    return nearby.astype(ml_dtypes.bfloat16), rows


def iota(shape, axis):
    return lax.broadcasted_iota(jnp.int32, shape, axis)


def halves(value):
    high = value.astype(BF16)
    return high, (value - high.astype(F32)).astype(BF16)


def whiten_kernel(x_ref, m_ref, table_ref, near_ref, rows_ref, out_ref, u_ref, re_ref, im_ref):
    q = pl.program_id(0)
    span = OWN * SLOT

    @pl.when(q == 0)
    def fold():
        for i in range(OWN):
            part = [
                x_ref[i, :, QUARTER * j : QUARTER * (j + 1)].astype(F32) for j in range(4)
            ]
            even, odd = part[0] + part[2], part[1] + part[3]
            kinds = (even + odd, even - odd, part[0] - part[2], part[1] - part[3])
            for kind, value in enumerate(kinds):
                high, low = halves(value)
                u_ref[kind, SLOT * i : SLOT * i + TRACES, :] = high
                u_ref[kind, span + SLOT * i : span + SLOT * i + TRACES, :] = low

    def times_table(kind):
        both = jnp.dot(u_ref[kind], table_ref[0], preferred_element_type=F32)
        return both[:span] + both[span:]

    @pl.when(q % 2 == 0)
    def real_class():
        both = times_table(q // 2)
        re_ref[q] = both[:, :CLASS]
        im_ref[q] = both[:, CLASS:]

    @pl.when(q % 2 == 1)
    def complex_class():
        sign = (2 - q).astype(F32)
        first, second = times_table(2), times_table(3)
        re_ref[q] = first[:, :CLASS] + sign * second[:, CLASS:]
        im_ref[q] = first[:, CLASS:] - sign * second[:, :CLASS]

    @pl.when(q == 3)
    def whiten():
        real = jnp.concatenate([re_ref[c] for c in range(4)], axis=1)
        imag = jnp.concatenate([im_ref[c] for c in range(4)], axis=1)
        magnitude = jnp.sqrt(real * real + imag * imag)
        high, low = halves(magnitude)
        near = near_ref[...]
        total = jnp.dot(high, near, preferred_element_type=F32) + jnp.dot(
            low, near, preferred_element_type=F32
        )
        level = total * rows_ref[1:2, :] + 1e-06
        weights = rows_ref[0:1, :] / level
        real = real * weights
        imag = imag * weights
        pieces = []
        for i in range(OWN):
            flags = m_ref[i : i + 1, :].astype(F32)
            square = (SLOT, TRACES)
            diagonal = iota(square, 0) == iota(square, 1)
            usable = jnp.sum(jnp.where(diagonal, flags, 0.0), axis=1, keepdims=True) > 0.5
            own_real = jnp.where(usable, real[SLOT * i : SLOT * (i + 1)], 0.0)
            own_imag = jnp.where(usable, imag[SLOT * i : SLOT * (i + 1)], 0.0)
            trace = iota((8, TRACES), 1)
            row = iota((8, TRACES), 0)
            spread = (
                (iota((TRACES, 128), 0) >> 3) == (iota((TRACES, 128), 1) & 7)
            ).astype(BF16)
            spare = []
            for shift in (4, 0):
                chosen = jnp.where((trace & 7) == ((row + shift) & 7), flags, 0.0)
                placed = jnp.dot(chosen.astype(BF16), spread, preferred_element_type=F32)
                spare.append(jnp.concatenate([placed] * (BINS // 128), axis=1))
            last = iota((8, BINS), 0) >= 4
            stack = jnp.concatenate(
                [
                    own_real[: SLOT - 8],
                    jnp.where(last, spare[0], own_real[SLOT - 8 :]),
                    own_imag[: SLOT - 8],
                    jnp.where(last, spare[1], own_imag[SLOT - 8 :]),
                ],
                axis=0,
            )
            pieces.append(jnp.transpose(stack).reshape(DEVICES, PER, 2 * SLOT))
        out_ref[...] = jnp.concatenate(pieces, axis=1).astype(BF16)


def whitened_spectra(traces, masks):
    near, rows = window_tables()
    return pl.pallas_call(
        whiten_kernel,
        grid=(4,),
        in_specs=[
            pl.BlockSpec((OWN, TRACES, SAMPLES), lambda q: (0, 0, 0)),
            pl.BlockSpec((OWN, TRACES), lambda q: (0, 0)),
            pl.BlockSpec((1, QUARTER, 2 * CLASS), lambda q: (q, 0, 0)),
            pl.BlockSpec((BINS, BINS), lambda q: (0, 0)),
            pl.BlockSpec((8, BINS), lambda q: (0, 0)),
        ],
        out_specs=pl.BlockSpec((DEVICES, OWN * PER, 2 * SLOT), lambda q: (0, 0, 0)),
        out_shape=jax.ShapeDtypeStruct((DEVICES, OWN * PER, 2 * SLOT), BF16),
        scratch_shapes=[
            pltpu.VMEM((4, 2 * OWN * SLOT, QUARTER), BF16),
            pltpu.VMEM((4, OWN * SLOT, CLASS), F32),
            pltpu.VMEM((4, OWN * SLOT, CLASS), F32),
        ],
        compiler_params=pltpu.CompilerParams(vmem_limit_bytes=48 * MIB),
        name="whiten",
    )(traces, masks, jnp.asarray(forward_tables()), jnp.asarray(near), jnp.asarray(rows))


def cross_kernel(got_ref, out_ref, own_ref, right_ref, flag_ref, part_ref):
    lanes = 2 * SLOT
    block = CHANNELS // COLS
    own_ref[...] = got_ref[...].reshape(DEVICES * OWN * PER, lanes).astype(F32)
    for i in range(OWN):
        for j in range(PER):
            value = own_ref[pl.ds(i * PER + j, DEVICES, stride=OWN * PER), :]
            for half in range(2):
                right_ref[j, pl.ds(half * CHANNELS + i, DEVICES, stride=OWN), :] = value
    lane = iota((CHANNELS, lanes), 1)
    spare = (lane & (SLOT - 1)) >= TRACES
    flags = jnp.zeros((CHANNELS, lanes), F32)
    for j in range(PER):
        value = jnp.where(spare, right_ref[j, :CHANNELS, :], 0.0)
        flags += pltpu.roll(value, 4 * j, 1) if j else value
    flag_ref[:CHANNELS] = flags
    flag_ref[CHANNELS:] = flags

    tile = (PER, lanes)
    row = iota(tile, 0)
    kept = (iota(tile, 1) & (SLOT - 1)) < TRACES
    sign = jnp.where(iota(tile, 1) < SLOT, 1.0, -1.0)

    def one_source(s, carry):
        start = pl.multiple_of((COLS - s) * block, 8)
        right = jnp.concatenate(
            [right_ref[j, pl.ds(start, CHANNELS), :] for j in range(PER)], axis=1
        ).astype(BF16)
        right_flags = flag_ref[pl.ds(start, CHANNELS), :].astype(BF16)
        left, left_flags = [], []
        for i in range(OWN):
            for r in range(ROWS):
                first = pl.multiple_of((r * COLS + s) * OWN * PER + i * PER, 8)
                value = jnp.where(kept, own_ref[pl.ds(first, PER), :], 0.0)
                turned = pltpu.roll(value, SLOT, 1) * sign
                both = []
                for j in range(PER):
                    keep = row == j
                    both.append(
                        jnp.concatenate(
                            [jnp.where(keep, value, 0.0), jnp.where(keep, turned, 0.0)], axis=0
                        )
                    )
                left.append(jnp.concatenate(both, axis=1).astype(BF16))
            left_flags.append(flag_ref[pl.ds(OWN * s + i, ROWS, stride=OWN * COLS), :])
        cross = lax.dot_general(
            jnp.concatenate(left, axis=0), right, NT, preferred_element_type=F32
        )
        tallies = lax.dot_general(
            jnp.concatenate(left_flags, axis=0).astype(BF16),
            right_flags,
            NT,
            preferred_element_type=F32,
        )
        scale = 1.0 / jnp.maximum(tallies, 1.0)
        stacked = cross.reshape(OWN * ROWS, 2 * PER, CHANNELS) * scale[:, None, :]
        part_ref[s] = stacked.astype(BF16)
        return carry

    lax.fori_loop(0, COLS, one_source, 0)

    where = iota((2 * PER, CHANNELS), 1) // block

    def one_row(g, carry):
        i = g // ROWS
        r = g % ROWS
        parts = [part_ref[s, g] for s in range(COLS)]
        for c in range(COLS):
            tiles = []
            for t in range(CHANNELS // 128):
                cut = slice(128 * t, 128 * (t + 1))
                places = range(128 * t // block, (128 * (t + 1) - 1) // block + 1)
                value = parts[(places[0] - c) % COLS][:, cut]
                for place in places[1:]:
                    value = jnp.where(
                        where[:, cut] == place, parts[(place - c) % COLS][:, cut], value
                    )
                tiles.append(value)
            lanes_of = pl.ds(pl.multiple_of(i * CHANNELS, 128), CHANNELS)
            out_ref[r * COLS + c, :, lanes_of] = jnp.concatenate(tiles, axis=1)
        return carry

    lax.fori_loop(0, OWN * ROWS, one_row, 0)


def cross_spectra(got):
    return pl.pallas_call(
        cross_kernel,
        out_shape=jax.ShapeDtypeStruct((DEVICES, 2 * PER, OWN * CHANNELS), BF16),
        scratch_shapes=[
            pltpu.VMEM((DEVICES * OWN * PER, 2 * SLOT), F32),
            pltpu.VMEM((PER, 2 * CHANNELS, 2 * SLOT), F32),
            pltpu.VMEM((2 * CHANNELS, 2 * SLOT), F32),
            pltpu.VMEM((COLS, OWN * ROWS, 2 * PER, CHANNELS), BF16),
        ],
        compiler_params=pltpu.CompilerParams(vmem_limit_bytes=48 * MIB),
        name="cross",
    )(got)


LAG_STEP = 512


def lag_kernel(col_ref, x_ref, table_ref, out_ref):
    block = CHANNELS // COLS
    turned = jnp.transpose(x_ref[...])

    def one_step(n, carry):
        lags = pl.ds(pl.multiple_of(n * LAG_STEP, LAG_STEP), LAG_STEP)
        value = jnp.dot(turned, table_ref[:, lags], preferred_element_type=F32)
        for place in range(COLS):
            source = (place + COLS - col_ref[0]) % COLS
            out_ref[source, 0, :, lags] = value[block * place : block * (place + 1)]
        return carry

    lax.fori_loop(0, LAGS // LAG_STEP, one_step, 0)


def correlations_of(stacked, col):
    block = CHANNELS // COLS
    return pl.pallas_call(
        lag_kernel,
        grid_spec=pltpu.PrefetchScalarGridSpec(
            num_scalar_prefetch=1,
            grid=(OWN,),
            in_specs=[
                pl.BlockSpec((2 * BINS, CHANNELS), lambda i, col: (0, i)),
                pl.BlockSpec((2 * BINS, LAGS), lambda i, col: (0, 0)),
            ],
            out_specs=pl.BlockSpec((COLS, 1, block, LAGS), lambda i, col: (0, i, 0, 0)),
        ),
        out_shape=jax.ShapeDtypeStruct((COLS, OWN, block, LAGS), F32),
        compiler_params=pltpu.CompilerParams(vmem_limit_bytes=48 * MIB),
        name="lags",
    )(col, stacked, jnp.asarray(lag_table()))


def local(traces, masks):
    axes = ("row", "col")
    spectra = whitened_spectra(traces, masks)
    by_bin = lax.all_to_all(spectra, axes, 0, 0, tiled=True)
    stacked = cross_spectra(by_bin)
    by_pair = lax.all_to_all(stacked, axes, 0, 0, tiled=True)
    col = lax.axis_index("col").astype(jnp.int32).reshape(1)
    result = correlations_of(by_pair.reshape(2 * BINS, OWN * CHANNELS), col)
    return result.reshape(OWN * COLS, CHANNELS // COLS, LAGS)


def solution(mesh):
    in_specs = (P(("row", "col"), None, None), P(("row", "col"), None))
    out_specs = P("row", "col", None)
    return jax.shard_map(local, mesh=mesh, in_specs=in_specs, out_specs=out_specs, check_vma=False)
```

time: 650 us -> 142 us (0.22)
  other arithmetic: 195 us -> 0 us
  waiting for transfers between devices: 227 us -> 57.6 us
  local copies, waits for them, and re-layouts: 97.3 us -> 7.1 us
  matrix products: 76.7 us -> 0 us
  Pallas kernels: 0 us -> 43.4 us
  between operations: 13.5 us -> 0.04 us
  blocking collectives: 38.8 us -> 27.9 us
    another operation x1 -> x0, other arithmetic: 136 us -> none
    psum x1 -> x0, waiting for transfers between devices: 132 us -> none  [from_root(): return lax.psum(block, axis)]
    all_gather x1 -> x0, waiting for transfers between devices: 94.4 us -> none  [local(): row_spec = lax.all_gather(spectra, 'col', axis=0, tiled=True)]
    dot_general x6 -> x0, matrix products: 76.7 us -> none  [the longest x1 21 us: local(): jnp.einsum('atf,btf->abf', left_imag, right_both, preferred_element_type=...]
    all_to_all x0 -> x1, waiting for transfers between devices: none -> 57.6 us  [local(): by_pair = lax.all_to_all(stacked, axes, 0, 0, tiled=True)]
    pallas_call x0 -> x3, Pallas kernels: none -> 43.4 us  [the longest x1 18.8 us: correlations_of(): pl.pallas_call(lag_kernel, grid_spec=pltpu.PrefetchScalarGridSpec(num_sca...]
    unnamed x10, local copies, waits for them, and re-layouts: 48.9 us -> 7.1 us
    cos x1 -> x0, other arithmetic: 35.4 us -> none  [lag_table(): jnp.cos(angles)]
  transfers between devices with their start and end apart: 2 -> 1, of which waited for: 2 -> 1; matrix products, arithmetic and copies ran while one was open for 14% -> 0% of each run, Pallas kernels for 0% -> 0%
where the time goes in v1:
time: 142 us; the launch traced here: 141 us
  waiting for transfers between devices  57.6 us (41%)
  Pallas kernels  43.4 us (31%)
  blocking collectives  27.9 us (20%)
  local copies, waits for them, and re-layouts  7.1 us (5%)
  starting transfers between devices  4.94 us (3%)
    all_to_all x1, waiting for transfers between devices, local(): by_pair = lax.all_to_all(stacked, axes, 0, 0, tiled=True)  57.6 us
    all_to_all x1, blocking collectives, local(): by_bin = lax.all_to_all(spectra, axes, 0, 0, tiled=True)  27.9 us
    pallas_call x1, Pallas kernels, correlations_of(): pl.pallas_call(lag_kernel, grid_spec=pltpu.PrefetchScalarGridSpec(num_sca...  18.8 us
    pallas_call x1, Pallas kernels, cross_spectra(): pl.pallas_call(cross_kernel, out_shape=jax.ShapeDtypeStruct((DEVICES, 2 *...  13.8 us
    pallas_call x1, Pallas kernels, whitened_spectra(): pl.pallas_call(whiten_kernel, grid=(4,), in_specs=[pl.BlockSpec((OWN, TRA...  10.9 us
    unnamed x10, local copies, waits for them, and re-layouts  7.1 us
    all_to_all x1, starting transfers between devices, local(): by_pair = lax.all_to_all(stacked, axes, 0, 0, tiled=True)  4.94 us
  transfers between devices with their start and end apart: 1, of which 1 were waited for; matrix products, arithmetic and copies ran while one was open for 0% of the time, Pallas kernels for 0%

profile of v1, /device:TPU:1, one launch (start us, length us, event | category | flops | bytes accessed | tf_op | source)
XLA Modules:
  0.0 140.9 jit_solution(13269641347020533724)
XLA Ops:
  0.0 0.0 copy-start.1
  0.0 1.9 %copy-done.1 = bf16[3,60,8192]{2,1,0:T(8,128)(2,1)S(1)} copy-done((bf16[3,60,8192]{2,1,0:T(8,128)(2,1)S(1)}, bf16[3,60,8192]{2,1,0:T(8,128)(2,1)}, u32[]{:S(2)}) %copy-start.1) | copy-done | bytes 2949144
  1.9 0.0 copy-start.2
  1.9 1.6 %copy-done.2 = bf16[1024,1024]{1,0:T(8,128)(2,1)S(1)} copy-done((bf16[1024,1024]{1,0:T(8,128)(2,1)S(1)}, bf16[1024,1024]{1,0:T(8,128)(2,1)}, u32[]{:S(2)}) %copy-start.2) | copy-done | bytes 2097176
  3.5 0.0 copy-start.3
  3.5 0.8 copy-done.3
  4.2 0.0 copy-start.4
  4.2 0.7 copy-done.4
  4.9 10.9 %whiten.1 = bf16[128,24,128]{2,1,0:T(8,128)(2,1)S(1)} custom-call(bf16[3,60,8192]{2,1,0:T(8,128)(2,1)S(1)} %copy-done.1, s32[3,60]{1,0:T(4,128)S(1)} %copy-done.4, bf16[4,2048,512]{2,1,0:T(8,128)(2,1)} %constant.12.clone.table_ref, bf16[1024,1024]{1,0:T(8,128)(2,1)S(1)} %copy-done.2, f32[8,1024]{1,0:T(8,128)S(1)} %copy-done.3), custom_call_target="tpu_custom_call" | custom-call | tf_op jit(solution)/shard_map/whiten/pallas_call | solution.py:169
  15.8 27.9 %all_to_all.10.got_ref = bf16[128,24,128]{2,1,0:T(8,128)(2,1)S(1)} all-to-all(bf16[128,24,128]{2,1,0:T(8,128)(2,1)S(1)} %whiten.1), channel_id=1, replica_groups=mesh['row'=8,'col'=16] {'row','col'}, dimensions={0} | all-to-all | bytes 1572864 | tf_op jit(solution)/shard_map/all_to_all | solution.py:331
  43.7 13.8 %cross.1 = bf16[128,16,1152]{2,1,0:T(8,128)(2,1)S(1)} custom-call(bf16[128,24,128]{2,1,0:T(8,128)(2,1)S(1)} %all_to_all.10.got_ref), custom_call_target="tpu_custom_call" | custom-call | tf_op jit(solution)/shard_map/cross/pallas_call | solution.py:277
  57.5 0.0 copy-start
  57.5 2.2 %copy-done = bf16[128,16,1152]{2,1,0:T(8,128)(2,1)} copy-done((bf16[128,16,1152]{2,1,0:T(8,128)(2,1)}, bf16[128,16,1152]{2,1,0:T(8,128)(2,1)S(1)}, u32[]{:S(2)}) %copy-start) | copy-done | bytes 4718616
  59.6 4.9 %all-to-all-start.1 = ((bf16[128,16,1152]{2,1,0:T(8,128)(2,1)}), bf16[128,16,1152]{2,1,0:T(8,128)(2,1)}, u32[]{:S(2)}, u32[]{:S(2)}) async-start(bf16[128,16,1152]{2,1,0:T(8,128)(2,1)} %copy-done), calls=%async_computation.1 | async-start | bytes 9437184 | tf_op jit(solution)/shard_map/all_to_all | solution.py:333
  64.6 57.6 %all-to-all-done.1 = bf16[128,16,1152]{2,1,0:T(8,128)(2,1)} async-done(((bf16[128,16,1152]{2,1,0:T(8,128)(2,1)}), bf16[128,16,1152]{2,1,0:T(8,128)(2,1)}, u32[]{:S(2)}, u32[]{:S(2)}) %all-to-all-start.1) | async-done | bytes 4718624 | tf_op jit(solution)/shard_map/all_to_all | solution.py:333
  122.2 18.8 %lags.1 = f32[16,3,24,2048]{3,2,1,0:T(8,128)} custom-call(s32[1]{0:T(128)} %bitcast.col_ref, bf16[2048,1152]{1,0:T(8,128)(2,1)} %bitcast.1.x_ref, bf16[2048,2048]{1,0:T(8,128)(2,1)} %constant.15.clone.table_ref), custom_call_target="tpu_custom_call" | custom-call | tf_op jit(solution)/shard_map/lags/pallas_call | solution.py:311
Async XLA Ops:
  0.0 1.9 %copy-start.1 = (bf16[3,60,8192]{2,1,0:T(8,128)(2,1)S(1)}, bf16[3,60,8192]{2,1,0:T(8,128)(2,1)}, u32[]{:S(2)}) copy-start(bf16[3,60,8192]{2,1,0:T(8,128)(2,1)} %x_ref.1) | copy-start | bytes 8847364
  1.9 1.6 %copy-start.2 = (bf16[1024,1024]{1,0:T(8,128)(2,1)S(1)}, bf16[1024,1024]{1,0:T(8,128)(2,1)}, u32[]{:S(2)}) copy-start(bf16[1024,1024]{1,0:T(8,128)(2,1)} %constant.13.clone.near_ref) | copy-start | bytes 6291460
  3.5 0.8 copy-start.3
  4.2 0.7 copy-start.4
  57.5 2.2 %copy-start = (bf16[128,16,1152]{2,1,0:T(8,128)(2,1)}, bf16[128,16,1152]{2,1,0:T(8,128)(2,1)S(1)}, u32[]{:S(2)}) copy-start(bf16[128,16,1152]{2,1,0:T(8,128)(2,1)S(1)} %cross.1) | copy-start | bytes 14155780
  59.6 62.5 %all-to-all-start.1 = ((bf16[128,16,1152]{2,1,0:T(8,128)(2,1)}), bf16[128,16,1152]{2,1,0:T(8,128)(2,1)}, u32[]{:S(2)}, u32[]{:S(2)}) async-start(bf16[128,16,1152]{2,1,0:T(8,128)(2,1)} %copy-done), calls=%async_computation.1 | async-start | bytes 9437184 | tf_op jit(solution)/shard_map/all_to_all | solution.py:333

commit v2 on v0

v2 whole, which is shorter than its diff:
```python
import math

import jax
import jax.numpy as jnp
import ml_dtypes
import numpy as np
from jax import lax
from jax.experimental import pallas as pl
from jax.experimental.pallas import tpu as pltpu
from jax.sharding import PartitionSpec as P

TRACES = 60
SAMPLES = 8192
BINS = 1024
LOW_BIN = 33
LAGS = 2048
SMOOTH = 64
EDGE = 64

F32 = jnp.float32
BF16 = jnp.bfloat16
MIB = 1 << 20

OWN = 3
SLOT = 64
QUARTER = SAMPLES // 4
CLASS = BINS // 4
PER = 8
DEVICES = BINS // PER
ROWS = 8
COLS = 16
CHANNELS = OWN * DEVICES
NT = (((1,), (1,)), ((), ()))


def bin_order():
    k = np.arange(BINS)
    return np.concatenate([k[(k + LOW_BIN) % 4 == q] for q in range(4)])


def angles_of(phases):
    return (phases % SAMPLES).astype(np.float32) * np.float32(2.0 * math.pi / SAMPLES)


def cosine(angles):
    return np.cos(angles.astype(np.float64)).astype(np.float32)


def sine(angles):
    return np.sin(angles.astype(np.float64)).astype(np.float32)


def forward_tables():
    bins = (LOW_BIN + bin_order()).reshape(4, 1, CLASS)
    angles = angles_of(np.arange(QUARTER).reshape(1, QUARTER, 1) * bins)
    return np.concatenate([cosine(angles), -sine(angles)], axis=2).astype(ml_dtypes.bfloat16)


def lag_tables():
    bins = LOW_BIN + bin_order()
    factor = np.float32(2.0 / math.sqrt(BINS))

    def at(lags):
        angles = angles_of(bins[:, None] * (lags[None, :] + SAMPLES))
        both = factor * np.stack([cosine(angles), -sine(angles)])
        return both.astype(ml_dtypes.bfloat16)

    edge = np.zeros((8, BINS), np.float32)
    edge[:2] = at(np.array([-LAGS // 2]))[:, :, 0].astype(np.float32)
    return at(np.arange(LAGS // 2)), edge


def window_tables():
    order = bin_order()
    nearby = np.abs(order[:, None] - order[None, :]) <= SMOOTH
    distance = np.minimum(order, BINS - 1 - order).astype(np.float32)
    ramp = np.minimum((distance + np.float32(0.5)) / np.float32(EDGE), np.float32(1.0))
    taper = np.float32(0.5) - np.float32(0.5) * cosine(np.float32(math.pi) * ramp)
    rows = np.zeros((8, BINS), np.float32)
    rows[0] = taper
    rows[1] = np.float32(1.0) / nearby.sum(axis=0).astype(np.float32)
    return nearby.astype(ml_dtypes.bfloat16), rows


def iota(shape, axis):
    return lax.broadcasted_iota(jnp.int32, shape, axis)


def halves(value):
    high = value.astype(BF16)
    return high, (value - high.astype(F32)).astype(BF16)


def whiten_kernel(
    x_hbm, m_hbm, table_hbm, near_hbm, rows_hbm, out_ref, x_ref, m_ref, table_ref, near_ref, rows_ref, u_ref, sems
):
    span = OWN * SLOT
    order = (0, 2, 1, 3)
    x_copies = [
        pltpu.make_async_copy(x_hbm.at[i], x_ref.at[i], sems.at[i]) for i in range(OWN)
    ]
    table_copies = {
        q: pltpu.make_async_copy(table_hbm.at[q], table_ref.at[q], sems.at[OWN + q]) for q in order
    }
    last_copies = [
        pltpu.make_async_copy(m_hbm, m_ref, sems.at[7]),
        pltpu.make_async_copy(rows_hbm, rows_ref, sems.at[8]),
        pltpu.make_async_copy(near_hbm, near_ref, sems.at[9]),
    ]
    for copy in (*x_copies, *table_copies.values(), *last_copies):
        copy.start()

    for i in range(OWN):
        x_copies[i].wait()
        part = [x_ref[i, :, QUARTER * j : QUARTER * (j + 1)].astype(F32) for j in range(4)]
        even, odd = part[0] + part[2], part[1] + part[3]
        kinds = (even + odd, even - odd, part[0] - part[2], part[1] - part[3])
        for kind, value in enumerate(kinds):
            high, low = halves(value)
            u_ref[kind, SLOT * i : SLOT * i + TRACES, :] = high
            u_ref[kind, span + SLOT * i : span + SLOT * i + TRACES, :] = low

    def times_table(kind, q):
        both = jnp.dot(u_ref[kind], table_ref[q], preferred_element_type=F32)
        both = both[:span] + both[span:]
        return both[:, :CLASS], both[:, CLASS:]

    reals, imags = {}, {}
    for q in order:
        table_copies[q].wait()
        if q % 2 == 0:
            reals[q], imags[q] = times_table(q // 2, q)
        else:
            first, second = times_table(2, q), times_table(3, q)
            if q == 1:
                reals[q], imags[q] = first[0] + second[1], first[1] - second[0]
            else:
                reals[q], imags[q] = first[0] - second[1], first[1] + second[0]
    for copy in last_copies:
        copy.wait()

    real = jnp.concatenate([reals[q] for q in range(4)], axis=1)
    imag = jnp.concatenate([imags[q] for q in range(4)], axis=1)
    magnitude = jnp.sqrt(real * real + imag * imag)
    near = near_ref[...]
    both = jnp.dot(
        jnp.concatenate(halves(magnitude), axis=0), near, preferred_element_type=F32
    )
    level = (both[:span] + both[span:]) * rows_ref[1:2, :] + 1e-06
    weights = rows_ref[0:1, :] / level
    real = real * weights
    imag = imag * weights
    pieces = []
    for i in range(OWN):
        flags = m_ref[i : i + 1, :].astype(F32)
        square = (SLOT, TRACES)
        diagonal = iota(square, 0) == iota(square, 1)
        usable = jnp.sum(jnp.where(diagonal, flags, 0.0), axis=1, keepdims=True) > 0.5
        own_real = jnp.where(usable, real[SLOT * i : SLOT * (i + 1)], 0.0)
        own_imag = jnp.where(usable, imag[SLOT * i : SLOT * (i + 1)], 0.0)
        trace = iota((8, TRACES), 1)
        row = iota((8, TRACES), 0)
        spread = ((iota((TRACES, 128), 0) >> 3) == (iota((TRACES, 128), 1) & 7)).astype(BF16)
        spare = []
        for shift in (4, 0):
            chosen = jnp.where((trace & 7) == ((row + shift) & 7), flags, 0.0)
            placed = jnp.dot(chosen.astype(BF16), spread, preferred_element_type=F32)
            spare.append(jnp.concatenate([placed] * (BINS // 128), axis=1))
        last = iota((8, BINS), 0) >= 4
        stack = jnp.concatenate(
            [
                own_real[: SLOT - 8],
                jnp.where(last, spare[0], own_real[SLOT - 8 :]),
                own_imag[: SLOT - 8],
                jnp.where(last, spare[1], own_imag[SLOT - 8 :]),
            ],
            axis=0,
        )
        pieces.append(jnp.transpose(stack).reshape(DEVICES, PER, 2 * SLOT))
    out_ref[...] = jnp.concatenate(pieces, axis=1).astype(BF16)


def anywhere(count):
    return [pl.BlockSpec(memory_space=pl.ANY)] * count


def whitened_spectra(traces, masks):
    near, rows = window_tables()
    return pl.pallas_call(
        whiten_kernel,
        in_specs=anywhere(5),
        out_shape=jax.ShapeDtypeStruct((DEVICES, OWN * PER, 2 * SLOT), BF16),
        scratch_shapes=[
            pltpu.VMEM((OWN, TRACES, SAMPLES), BF16),
            pltpu.VMEM((OWN, TRACES), jnp.int32),
            pltpu.VMEM((4, QUARTER, 2 * CLASS), BF16),
            pltpu.VMEM((BINS, BINS), BF16),
            pltpu.VMEM((8, BINS), F32),
            pltpu.VMEM((4, 2 * OWN * SLOT, QUARTER), BF16),
            pltpu.SemaphoreType.DMA((10,)),
        ],
        compiler_params=pltpu.CompilerParams(vmem_limit_bytes=60 * MIB),
        name="whiten",
    )(traces, masks, jnp.asarray(forward_tables()), jnp.asarray(near), jnp.asarray(rows))


def cross_kernel(got_ref, out_hbm, own_ref, sorted_ref, scale_ref, part_ref, merged_ref, sems):
    lanes = 2 * SLOT
    block = CHANNELS // COLS
    own_ref[...] = got_ref[...].reshape(DEVICES * OWN * PER, lanes).astype(F32)
    lane = iota((CHANNELS, lanes), 1)
    spare = (lane & (SLOT - 1)) >= TRACES
    sign = jnp.where(lane < SLOT, 1.0, -1.0)
    flags = jnp.zeros((CHANNELS, lanes), F32)
    for j in range(PER):
        for i in range(OWN):
            value = own_ref[pl.ds(i * PER + j, DEVICES, stride=OWN * PER), :]
            sorted_ref[j, pl.ds(i, DEVICES, stride=OWN), :] = value
        extra = jnp.where(spare, sorted_ref[j], 0.0)
        flags += pltpu.roll(extra, 4 * j, 1) if j else extra
    flags = flags.astype(BF16)
    tallies = lax.dot_general(flags, flags, NT, preferred_element_type=F32)
    scale_ref[...] = 1.0 / jnp.maximum(tallies, 1.0)
    for j in range(PER):
        right = sorted_ref[j]
        left = jnp.where(spare, 0.0, right)
        left = jnp.concatenate([left, pltpu.roll(left, SLOT, 1) * sign], axis=0)
        cross = lax.dot_general(
            left.astype(BF16), right.astype(BF16), NT, preferred_element_type=F32
        )
        for t in range(CHANNELS // 128):
            for p in range(2):
                part_ref[t, pl.ds(PER * p + j, CHANNELS, stride=2 * PER), :] = (
                    cross[CHANNELS * p : CHANNELS * (p + 1), 128 * t : 128 * (t + 1)]
                    * scale_ref[:, 128 * t : 128 * (t + 1)]
                )

    def copy_out(g):
        return pltpu.make_async_copy(
            merged_ref.at[g],
            out_hbm.at[
                pl.ds((g % ROWS) * COLS, COLS),
                :,
                pl.ds(pl.multiple_of(g // ROWS * CHANNELS, 128), CHANNELS),
            ],
            sems.at[g],
        )

    where = iota((2 * PER, CHANNELS), 1) // block
    bits = [(where >> k) & 1 == 1 for k in range(4)]

    def one_row(g, carry):
        parts = []
        for s in range(COLS):
            channel = (g % ROWS) * OWN * COLS + OWN * s + g // ROWS
            rows = pl.ds(pl.multiple_of(channel * 2 * PER, 2 * PER), 2 * PER)
            value = jnp.concatenate(
                [part_ref[t, rows, :] for t in range(CHANNELS // 128)], axis=1
            )
            value = value.astype(BF16)
            parts.append(pltpu.roll(value, block * s, 1) if s else value)
        for t in range(CHANNELS // 128):
            cut = slice(128 * t, 128 * (t + 1))
            tiles = [part[:, cut] for part in parts]
            for k in range(4):
                tiles = [
                    jnp.where(bits[k][:, cut], tiles[(s + (1 << k)) % COLS], tiles[s])
                    for s in range(COLS)
                ]
            for c in range(COLS):
                merged_ref[g, c, :, cut] = tiles[-c % COLS]
        copy_out(g).start()
        return carry

    lax.fori_loop(0, OWN * ROWS, one_row, 0, unroll=3)

    def one_wait(g, carry):
        copy_out(g).wait()
        return carry

    lax.fori_loop(0, OWN * ROWS, one_wait, 0)


def cross_spectra(got):
    return pl.pallas_call(
        cross_kernel,
        out_specs=pl.BlockSpec(memory_space=pl.ANY),
        out_shape=jax.ShapeDtypeStruct((DEVICES, 2 * PER, OWN * CHANNELS), BF16),
        scratch_shapes=[
            pltpu.VMEM((DEVICES * OWN * PER, 2 * SLOT), F32),
            pltpu.VMEM((PER, CHANNELS, 2 * SLOT), F32),
            pltpu.VMEM((CHANNELS, CHANNELS), F32),
            pltpu.VMEM((CHANNELS // 128, CHANNELS * 2 * PER, 128), F32),
            pltpu.VMEM((OWN * ROWS, COLS, 2 * PER, CHANNELS), BF16),
            pltpu.SemaphoreType.DMA((OWN * ROWS,)),
        ],
        compiler_params=pltpu.CompilerParams(vmem_limit_bytes=60 * MIB),
        name="cross",
    )(got)


LAG_STEP = 256
HALF = LAGS // 2


def lag_kernel(col_ref, x_hbm, table_hbm, edge_ref, out_hbm, x_ref, table_ref, out_ref, sems):
    block = CHANNELS // COLS
    steps = HALF // LAG_STEP
    x_copies = [
        pltpu.make_async_copy(
            x_hbm.at[:, :, pl.ds(CHANNELS * i, CHANNELS)], x_ref.at[i], sems.at[i]
        )
        for i in range(OWN)
    ]
    table_copies = [
        pltpu.make_async_copy(table_hbm.at[n], table_ref.at[n], sems.at[OWN + n])
        for n in range(steps)
    ]
    x_copies[0].start()
    for n in reversed(range(steps)):
        table_copies[n].start()
    for i in range(1, OWN):
        x_copies[i].start()

    def store(i, first, value):
        width = value.shape[1]
        for place in range(COLS):
            source = (place + COLS - col_ref[0]) % COLS
            out_ref[i, source, :, first : first + width] = value[block * place : block * (place + 1)]

    copies = []

    def send(i, first):
        copy = pltpu.make_async_copy(
            out_ref.at[i, :, :, pl.ds(first, LAG_STEP)],
            out_hbm.at[:, i, :, pl.ds(first, LAG_STEP)],
            sems.at[OWN + steps + len(copies)],
        )
        copy.start()
        copies.append(copy)

    lane = iota((CHANNELS, 128), 1)
    mirror = (128 - lane) & 127
    for i in range(OWN):
        x_copies[i].wait()
        parts = []
        for p in range(2):
            rows = x_ref[i, :, PER * p : PER * (p + 1), :].astype(F32).reshape(BINS, CHANNELS)
            parts.append(jnp.transpose(rows))
        edge = jnp.sum(
            parts[0] * edge_ref[0:1, :] + parts[1] * edge_ref[1:2, :], axis=1, keepdims=True
        )
        real, imag = parts[0].astype(BF16), parts[1].astype(BF16)
        before = jnp.broadcast_to(edge, (CHANNELS, 128))
        for n in reversed(range(steps)):
            if i == 0:
                table_copies[n].wait()
            even = jnp.dot(real, table_ref[n, 0], preferred_element_type=F32)
            odd = jnp.dot(imag, table_ref[n, 1], preferred_element_type=F32)
            store(i, HALF + LAG_STEP * n, even + odd)
            send(i, HALF + LAG_STEP * n)
            back = even - odd
            for t in reversed(range(LAG_STEP // 128)):
                turned = jnp.take_along_axis(back[:, 128 * t : 128 * (t + 1)], mirror, axis=1)
                first = HALF - LAG_STEP * n - 128 * (t + 1)
                store(i, first, jnp.where(lane == 0, before, turned))
                before = turned
            send(i, HALF - LAG_STEP * (n + 1))
    for copy in copies:
        copy.wait()


def correlations_of(stacked, col):
    block = CHANNELS // COLS
    steps = HALF // LAG_STEP
    table, edge = lag_tables()
    table = table.reshape(2, BINS, steps, LAG_STEP).transpose(2, 0, 1, 3)
    return pl.pallas_call(
        lag_kernel,
        in_specs=[
            pl.BlockSpec(memory_space=pltpu.SMEM),
            *anywhere(2),
            pl.BlockSpec(memory_space=pltpu.VMEM),
        ],
        out_specs=pl.BlockSpec(memory_space=pl.ANY),
        out_shape=jax.ShapeDtypeStruct((COLS, OWN, block, LAGS), F32),
        scratch_shapes=[
            pltpu.VMEM((OWN, DEVICES, 2 * PER, CHANNELS), BF16),
            pltpu.VMEM((steps, 2, BINS, LAG_STEP), BF16),
            pltpu.VMEM((OWN, COLS, block, LAGS), F32),
            pltpu.SemaphoreType.DMA((OWN + steps + 2 * OWN * steps,)),
        ],
        compiler_params=pltpu.CompilerParams(vmem_limit_bytes=60 * MIB),
        name="lags",
    )(col, stacked, jnp.asarray(table), jnp.asarray(edge))


def local(traces, masks):
    axes = ("row", "col")
    spectra = whitened_spectra(traces, masks)
    by_bin = lax.all_to_all(spectra, axes, 0, 0, tiled=True)
    stacked = cross_spectra(by_bin)
    by_pair = lax.all_to_all(stacked, axes, 0, 0, tiled=True)
    col = lax.axis_index("col").astype(jnp.int32).reshape(1)
    result = correlations_of(by_pair, col)
    return result.reshape(OWN * COLS, CHANNELS // COLS, LAGS)


def solution(mesh):
    in_specs = (P(("row", "col"), None, None), P(("row", "col"), None))
    out_specs = P("row", "col", None)
    return jax.shard_map(local, mesh=mesh, in_specs=in_specs, out_specs=out_specs, check_vma=False)
```

time: 650 us -> 125 us (0.19)
  other arithmetic: 195 us -> 0 us
  waiting for transfers between devices: 227 us -> 57.6 us
  local copies, waits for them, and re-layouts: 97.3 us -> 0 us
  matrix products: 76.7 us -> 0 us
  Pallas kernels: 0 us -> 33.7 us
  between operations: 13.5 us -> 0.19 us
  blocking collectives: 38.8 us -> 28.2 us
    another operation x1 -> x0, other arithmetic: 136 us -> none
    psum x1 -> x0, waiting for transfers between devices: 132 us -> none  [from_root(): return lax.psum(block, axis)]
    all_gather x1 -> x0, waiting for transfers between devices: 94.4 us -> none  [local(): row_spec = lax.all_gather(spectra, 'col', axis=0, tiled=True)]
    dot_general x6 -> x0, matrix products: 76.7 us -> none  [the longest x1 21 us: local(): jnp.einsum('atf,btf->abf', left_imag, right_both, preferred_element_type=...]
    all_to_all x0 -> x1, waiting for transfers between devices: none -> 57.6 us  [local(): by_pair = lax.all_to_all(stacked, axes, 0, 0, tiled=True)]
    unnamed x10 -> x0, local copies, waits for them, and re-layouts: 48.9 us -> none
    cos x1 -> x0, other arithmetic: 35.4 us -> none  [lag_table(): jnp.cos(angles)]
    pallas_call x0 -> x3, Pallas kernels: none -> 33.7 us  [the longest x1 12.4 us: correlations_of(): pl.pallas_call(lag_kernel, in_specs=[pl.BlockSpec(memory_space=pltpu.SMEM...]
  transfers between devices with their start and end apart: 2 -> 1, of which waited for: 2 -> 1; matrix products, arithmetic and copies ran while one was open for 14% -> 0% of each run, Pallas kernels for 0% -> 0%
where the time goes in v2:
time: 125 us
  waiting for transfers between devices  57.6 us (46%)
  Pallas kernels  33.7 us (27%)
  blocking collectives  28.2 us (23%)
  starting transfers between devices  5.11 us (4%)
    all_to_all x1, waiting for transfers between devices, local(): by_pair = lax.all_to_all(stacked, axes, 0, 0, tiled=True)  57.6 us
    all_to_all x1, blocking collectives, local(): by_bin = lax.all_to_all(spectra, axes, 0, 0, tiled=True)  28.2 us
    pallas_call x1, Pallas kernels, correlations_of(): pl.pallas_call(lag_kernel, in_specs=[pl.BlockSpec(memory_space=pltpu.SMEM...  12.4 us
    pallas_call x1, Pallas kernels, whitened_spectra(): pl.pallas_call(whiten_kernel, in_specs=anywhere(5), out_shape=jax.ShapeDt...  12.4 us
    pallas_call x1, Pallas kernels, cross_spectra(): pl.pallas_call(cross_kernel, out_specs=pl.BlockSpec(memory_space=pl.ANY),...  8.8 us
    all_to_all x1, starting transfers between devices, local(): by_pair = lax.all_to_all(stacked, axes, 0, 0, tiled=True)  5.11 us
  transfers between devices with their start and end apart: 1, of which 1 were waited for; matrix products, arithmetic and copies ran while one was open for 0% of the time, Pallas kernels for 0%

profile of v2, /device:TPU:1, one launch (start us, length us, event | category | flops | bytes accessed | tf_op | source)
XLA Modules:
  0.0 124.8 jit_solution(16072109362937203035)
XLA Ops:
  0.0 12.4 %whiten.1 = bf16[128,24,128]{2,1,0:T(8,128)(2,1)} custom-call(bf16[3,60,8192]{2,1,0:T(8,128)(2,1)} %x_hbm.1, s32[3,60]{1,0:T(4,128)} %m_hbm.1, bf16[4,2048,512]{2,1,0:T(8,128)(2,1)} %constant.14.clone.table_hbm, bf16[1024,1024]{1,0:T(8,128)(2,1)} %constant.15.clone.near_hbm, f32[8,1024]{1,0:T(8,128)} %constant.16.clone.rows_hbm), custom_call_target="tpu_custom_call" | custom-call | tf_op jit(solution)/shard_map/whiten/pallas_call | solution.py:189
  12.4 28.2 %all_to_all.10.got_ref = bf16[128,24,128]{2,1,0:T(8,128)(2,1)} all-to-all(bf16[128,24,128]{2,1,0:T(8,128)(2,1)} %whiten.1), channel_id=1, replica_groups=mesh['row'=8,'col'=16] {'row','col'}, dimensions={0} | all-to-all | bytes 1572864 | tf_op jit(solution)/shard_map/all_to_all | solution.py:401
  40.6 8.8 %cross.1 = bf16[128,16,1152]{2,1,0:T(8,128)(2,1)} custom-call(bf16[128,24,128]{2,1,0:T(8,128)(2,1)} %all_to_all.10.got_ref), custom_call_target="tpu_custom_call" | custom-call | tf_op jit(solution)/shard_map/cross/pallas_call | solution.py:285
  49.4 5.1 %all-to-all-start.1 = ((bf16[128,16,1152]{2,1,0:T(8,128)(2,1)}), bf16[128,16,1152]{2,1,0:T(8,128)(2,1)}, u32[]{:S(2)}, u32[]{:S(2)}) async-start(bf16[128,16,1152]{2,1,0:T(8,128)(2,1)} %cross.1), calls=%async_computation.1 | async-start | bytes 9437184 | tf_op jit(solution)/shard_map/all_to_all | solution.py:403
  54.5 57.6 %all-to-all-done.1.x_hbm = bf16[128,16,1152]{2,1,0:T(8,128)(2,1)} async-done(((bf16[128,16,1152]{2,1,0:T(8,128)(2,1)}), bf16[128,16,1152]{2,1,0:T(8,128)(2,1)}, u32[]{:S(2)}, u32[]{:S(2)}) %all-to-all-start.1) | async-done | bytes 4718624 | tf_op jit(solution)/shard_map/all_to_all | solution.py:403
  112.2 12.4 %lags.1 = f32[16,3,24,2048]{3,2,1,0:T(8,128)} custom-call(s32[1]{0:T(128)} %bitcast.col_ref, bf16[128,16,1152]{2,1,0:T(8,128)(2,1)} %all-to-all-done.1.x_hbm, bf16[4,2,1024,256]{3,2,1,0:T(8,128)(2,1)} %constant.17.clone.table_hbm, f32[8,1024]{1,0:T(8,128)} %constant.18.clone.edge_ref), custom_call_target="tpu_custom_call" | custom-call | tf_op jit(solution)/shard_map/lags/pallas_call | solution.py:378
Async XLA Ops:
  49.4 62.7 %all-to-all-start.1 = ((bf16[128,16,1152]{2,1,0:T(8,128)(2,1)}), bf16[128,16,1152]{2,1,0:T(8,128)(2,1)}, u32[]{:S(2)}, u32[]{:S(2)}) async-start(bf16[128,16,1152]{2,1,0:T(8,128)(2,1)} %cross.1), calls=%async_computation.1 | async-start | bytes 9437184 | tf_op jit(solution)/shard_map/all_to_all | solution.py:403

commit v3 on v2

--- a/solution.py
+++ b/solution.py
@@ -70,7 +70,7 @@
     return at(np.arange(LAGS // 2)), edge
 
 
-def window_tables():
+def window_rows():
     order = bin_order()
     nearby = np.abs(order[:, None] - order[None, :]) <= SMOOTH
     distance = np.minimum(order, BINS - 1 - order).astype(np.float32)
@@ -79,7 +79,7 @@
     rows = np.zeros((8, BINS), np.float32)
     rows[0] = taper
     rows[1] = np.float32(1.0) / nearby.sum(axis=0).astype(np.float32)
-    return nearby.astype(ml_dtypes.bfloat16), rows
+    return rows
 
 
 def iota(shape, axis):
@@ -92,7 +92,7 @@
 
 
 def whiten_kernel(
-    x_hbm, m_hbm, table_hbm, near_hbm, rows_hbm, out_ref, x_ref, m_ref, table_ref, near_ref, rows_ref, u_ref, sems
+    x_hbm, m_hbm, table_hbm, rows_hbm, out_ref, x_ref, m_ref, table_ref, rows_ref, u_ref, sems
 ):
     span = OWN * SLOT
     order = (0, 2, 1, 3)
@@ -105,13 +105,13 @@
     last_copies = [
         pltpu.make_async_copy(m_hbm, m_ref, sems.at[7]),
         pltpu.make_async_copy(rows_hbm, rows_ref, sems.at[8]),
-        pltpu.make_async_copy(near_hbm, near_ref, sems.at[9]),
     ]
     for copy in (*x_copies, *table_copies.values(), *last_copies):
         copy.start()
+    for copy in x_copies:
+        copy.wait()
 
     for i in range(OWN):
-        x_copies[i].wait()
         part = [x_ref[i, :, QUARTER * j : QUARTER * (j + 1)].astype(F32) for j in range(4)]
         even, odd = part[0] + part[2], part[1] + part[3]
         kinds = (even + odd, even - odd, part[0] - part[2], part[1] - part[3])
@@ -127,7 +127,12 @@
 
     reals, imags = {}, {}
     for q in order:
-        table_copies[q].wait()
+        if q == 0:
+            table_copies[0].wait()
+            table_copies[2].wait()
+        if q == 1:
+            for copy in (table_copies[1], table_copies[3], *last_copies):
+                copy.wait()
         if q % 2 == 0:
             reals[q], imags[q] = times_table(q // 2, q)
         else:
@@ -136,17 +141,30 @@
                 reals[q], imags[q] = first[0] + second[1], first[1] - second[0]
             else:
                 reals[q], imags[q] = first[0] - second[1], first[1] + second[0]
-    for copy in last_copies:
-        copy.wait()
-
+
+    place = {c: (c - LOW_BIN) % 4 for c in range(4)}
+    by_place = sorted(range(4), key=place.get)
+    sizes = {c: jnp.sqrt(reals[c] * reals[c] + imags[c] * imags[c]) for c in range(4)}
+    every = sizes[0] + sizes[1] + sizes[2] + sizes[3]
+    reach = SMOOTH // 4
+    band = jnp.abs(iota((CLASS, CLASS), 0) - iota((CLASS, CLASS), 1)) < reach
+    middle = jnp.dot(
+        jnp.concatenate(halves(every), axis=0), band.astype(BF16), preferred_element_type=F32
+    )
+    middle = middle[:span] + middle[span:]
+    lane = iota((span, CLASS), 1)
+    totals = {}
+    upto = jnp.zeros((span, CLASS), F32)
+    for c in by_place:
+        onward = every - upto
+        upto = upto + sizes[c]
+        ahead = jnp.where(lane < CLASS - reach, pltpu.roll(upto, CLASS - reach, 1), 0.0)
+        behind = jnp.where(lane >= reach, pltpu.roll(onward, reach, 1), 0.0)
+        totals[c] = middle + ahead + behind
+    total = jnp.concatenate([totals[c] for c in range(4)], axis=1)
     real = jnp.concatenate([reals[q] for q in range(4)], axis=1)
     imag = jnp.concatenate([imags[q] for q in range(4)], axis=1)
-    magnitude = jnp.sqrt(real * real + imag * imag)
-    near = near_ref[...]
-    both = jnp.dot(
-        jnp.concatenate(halves(magnitude), axis=0), near, preferred_element_type=F32
-    )
-    level = (both[:span] + both[span:]) * rows_ref[1:2, :] + 1e-06
+    level = total * rows_ref[1:2, :] + 1e-06
     weights = rows_ref[0:1, :] / level
     real = real * weights
     imag = imag * weights
@@ -185,26 +203,24 @@
 
 
 def whitened_spectra(traces, masks):
-    near, rows = window_tables()
     return pl.pallas_call(
         whiten_kernel,
-        in_specs=anywhere(5),
+        in_specs=anywhere(4),
         out_shape=jax.ShapeDtypeStruct((DEVICES, OWN * PER, 2 * SLOT), BF16),
         scratch_shapes=[
             pltpu.VMEM((OWN, TRACES, SAMPLES), BF16),
             pltpu.VMEM((OWN, TRACES), jnp.int32),
             pltpu.VMEM((4, QUARTER, 2 * CLASS), BF16),
-            pltpu.VMEM((BINS, BINS), BF16),
             pltpu.VMEM((8, BINS), F32),
             pltpu.VMEM((4, 2 * OWN * SLOT, QUARTER), BF16),
-            pltpu.SemaphoreType.DMA((10,)),
+            pltpu.SemaphoreType.DMA((9,)),
         ],
         compiler_params=pltpu.CompilerParams(vmem_limit_bytes=60 * MIB),
         name="whiten",
-    )(traces, masks, jnp.asarray(forward_tables()), jnp.asarray(near), jnp.asarray(rows))
-
-
-def cross_kernel(got_ref, out_hbm, own_ref, sorted_ref, scale_ref, part_ref, merged_ref, sems):
+    )(traces, masks, jnp.asarray(forward_tables()), jnp.asarray(window_rows()))
+
+
+def cross_kernel(got_ref, out_ref, own_ref, sorted_ref, scale_ref, part_ref):
     lanes = 2 * SLOT
     block = CHANNELS // COLS
     own_ref[...] = got_ref[...].reshape(DEVICES * OWN * PER, lanes).astype(F32)
@@ -235,17 +251,6 @@
                     * scale_ref[:, 128 * t : 128 * (t + 1)]
                 )
 
-    def copy_out(g):
-        return pltpu.make_async_copy(
-            merged_ref.at[g],
-            out_hbm.at[
-                pl.ds((g % ROWS) * COLS, COLS),
-                :,
-                pl.ds(pl.multiple_of(g // ROWS * CHANNELS, 128), CHANNELS),
-            ],
-            sems.at[g],
-        )
-
     where = iota((2 * PER, CHANNELS), 1) // block
     bits = [(where >> k) & 1 == 1 for k in range(4)]
 
@@ -268,64 +273,41 @@
                     for s in range(COLS)
                 ]
             for c in range(COLS):
-                merged_ref[g, c, :, cut] = tiles[-c % COLS]
-        copy_out(g).start()
+                lanes_of = pl.ds(pl.multiple_of(g // ROWS * CHANNELS + 128 * t, 128), 128)
+                out_ref[g % ROWS * COLS + c, :, lanes_of] = tiles[-c % COLS]
         return carry
 
     lax.fori_loop(0, OWN * ROWS, one_row, 0, unroll=3)
-
-    def one_wait(g, carry):
-        copy_out(g).wait()
-        return carry
-
-    lax.fori_loop(0, OWN * ROWS, one_wait, 0)
 
 
 def cross_spectra(got):
     return pl.pallas_call(
         cross_kernel,
-        out_specs=pl.BlockSpec(memory_space=pl.ANY),
         out_shape=jax.ShapeDtypeStruct((DEVICES, 2 * PER, OWN * CHANNELS), BF16),
         scratch_shapes=[
             pltpu.VMEM((DEVICES * OWN * PER, 2 * SLOT), F32),
             pltpu.VMEM((PER, CHANNELS, 2 * SLOT), F32),
             pltpu.VMEM((CHANNELS, CHANNELS), F32),
             pltpu.VMEM((CHANNELS // 128, CHANNELS * 2 * PER, 128), F32),
-            pltpu.VMEM((OWN * ROWS, COLS, 2 * PER, CHANNELS), BF16),
-            pltpu.SemaphoreType.DMA((OWN * ROWS,)),
         ],
-        compiler_params=pltpu.CompilerParams(vmem_limit_bytes=60 * MIB),
+        compiler_params=pltpu.CompilerParams(vmem_limit_bytes=32 * MIB),
         name="cross",
     )(got)
 
 
-LAG_STEP = 256
+LAG_STEP = 512
 HALF = LAGS // 2
 
 
-def lag_kernel(col_ref, x_hbm, table_hbm, edge_ref, out_hbm, x_ref, table_ref, out_ref, sems):
+def lag_kernel(x_ref, table_ref, edge_ref, out_hbm, out_ref, sems):
     block = CHANNELS // COLS
     steps = HALF // LAG_STEP
-    x_copies = [
-        pltpu.make_async_copy(
-            x_hbm.at[:, :, pl.ds(CHANNELS * i, CHANNELS)], x_ref.at[i], sems.at[i]
-        )
-        for i in range(OWN)
-    ]
-    table_copies = [
-        pltpu.make_async_copy(table_hbm.at[n], table_ref.at[n], sems.at[OWN + n])
-        for n in range(steps)
-    ]
-    x_copies[0].start()
-    for n in reversed(range(steps)):
-        table_copies[n].start()
-    for i in range(1, OWN):
-        x_copies[i].start()
+    col = lax.axis_index("col")
 
     def store(i, first, value):
         width = value.shape[1]
         for place in range(COLS):
-            source = (place + COLS - col_ref[0]) % COLS
+            source = (place + COLS - col) % COLS
             out_ref[i, source, :, first : first + width] = value[block * place : block * (place + 1)]
 
     copies = []
@@ -334,7 +316,7 @@
         copy = pltpu.make_async_copy(
             out_ref.at[i, :, :, pl.ds(first, LAG_STEP)],
             out_hbm.at[:, i, :, pl.ds(first, LAG_STEP)],
-            sems.at[OWN + steps + len(copies)],
+            sems.at[len(copies)],
         )
         copy.start()
         copies.append(copy)
@@ -342,10 +324,10 @@
     lane = iota((CHANNELS, 128), 1)
     mirror = (128 - lane) & 127
     for i in range(OWN):
-        x_copies[i].wait()
         parts = []
         for p in range(2):
-            rows = x_ref[i, :, PER * p : PER * (p + 1), :].astype(F32).reshape(BINS, CHANNELS)
+            rows = x_ref[:, PER * p : PER * (p + 1), CHANNELS * i : CHANNELS * (i + 1)]
+            rows = rows.astype(F32).reshape(BINS, CHANNELS)
             parts.append(jnp.transpose(rows))
         edge = jnp.sum(
             parts[0] * edge_ref[0:1, :] + parts[1] * edge_ref[1:2, :], axis=1, keepdims=True
@@ -353,8 +335,6 @@
         real, imag = parts[0].astype(BF16), parts[1].astype(BF16)
         before = jnp.broadcast_to(edge, (CHANNELS, 128))
         for n in reversed(range(steps)):
-            if i == 0:
-                table_copies[n].wait()
             even = jnp.dot(real, table_ref[n, 0], preferred_element_type=F32)
             odd = jnp.dot(imag, table_ref[n, 1], preferred_element_type=F32)
             store(i, HALF + LAG_STEP * n, even + odd)
@@ -370,29 +350,30 @@
         copy.wait()
 
 
-def correlations_of(stacked, col):
+def split_lag_tables():
+    table, edge = lag_tables()
+    steps = HALF // LAG_STEP
+    table = table.reshape(2, BINS, steps, LAG_STEP).transpose(2, 0, 1, 3)
+    return jnp.asarray(table), jnp.asarray(edge)
+
+
+def correlations_of(stacked, table, edge):
     block = CHANNELS // COLS
     steps = HALF // LAG_STEP
-    table, edge = lag_tables()
-    table = table.reshape(2, BINS, steps, LAG_STEP).transpose(2, 0, 1, 3)
     return pl.pallas_call(
         lag_kernel,
         in_specs=[
-            pl.BlockSpec(memory_space=pltpu.SMEM),
-            *anywhere(2),
-            pl.BlockSpec(memory_space=pltpu.VMEM),
+            *[pl.BlockSpec(memory_space=pltpu.VMEM)] * 3,
         ],
         out_specs=pl.BlockSpec(memory_space=pl.ANY),
         out_shape=jax.ShapeDtypeStruct((COLS, OWN, block, LAGS), F32),
         scratch_shapes=[
-            pltpu.VMEM((OWN, DEVICES, 2 * PER, CHANNELS), BF16),
-            pltpu.VMEM((steps, 2, BINS, LAG_STEP), BF16),
             pltpu.VMEM((OWN, COLS, block, LAGS), F32),
-            pltpu.SemaphoreType.DMA((OWN + steps + 2 * OWN * steps,)),
+            pltpu.SemaphoreType.DMA((2 * OWN * steps,)),
         ],
-        compiler_params=pltpu.CompilerParams(vmem_limit_bytes=60 * MIB),
+        compiler_params=pltpu.CompilerParams(vmem_limit_bytes=36 * MIB),
         name="lags",
-    )(col, stacked, jnp.asarray(table), jnp.asarray(edge))
+    )(stacked, table, edge)
 
 
 def local(traces, masks):
@@ -400,9 +381,9 @@
     spectra = whitened_spectra(traces, masks)
     by_bin = lax.all_to_all(spectra, axes, 0, 0, tiled=True)
     stacked = cross_spectra(by_bin)
+    table, edge = split_lag_tables()
     by_pair = lax.all_to_all(stacked, axes, 0, 0, tiled=True)
-    col = lax.axis_index("col").astype(jnp.int32).reshape(1)
-    result = correlations_of(by_pair, col)
+    result = correlations_of(by_pair, table, edge)
     return result.reshape(OWN * COLS, CHANNELS // COLS, LAGS)
 
 

time: 125 us -> 118 us (0.944)
  blocking collectives: 28.2 us -> 91.4 us
  waiting for transfers between devices: 57.6 us -> 0 us
  Pallas kernels: 33.7 us -> 26.2 us
  starting transfers between devices: 5.11 us -> 0 us
    all_to_all x0 -> x1, blocking collectives: none -> 63.3 us  [local(): by_pair = lax.all_to_all(stacked, axes, 0, 0, tiled=True)]
    all_to_all x1 -> x0, waiting for transfers between devices: 57.6 us -> none  [local(): by_pair = lax.all_to_all(stacked, axes, 0, 0, tiled=True)]
    pallas_call x3, Pallas kernels: 33.7 us -> 26.2 us  [the longest x1 10.5 us: whitened_spectra(): pl.pallas_call(whiten_kernel, in_specs=anywhere(4), out_shape=jax.ShapeDt...]
    all_to_all x1 -> x0, starting transfers between devices: 5.11 us -> none  [local(): by_pair = lax.all_to_all(stacked, axes, 0, 0, tiled=True)]
  transfers between devices with their start and end apart: 1 -> 0, of which waited for: 1 -> 0; matrix products, arithmetic and copies ran while one was open for 0% -> 0% of each run, Pallas kernels for 0% -> 0%
where the time goes in v3:
time: 118 us
  blocking collectives  91.4 us (77%)
  Pallas kernels  26.2 us (22%)
    all_to_all x1, blocking collectives, local(): by_pair = lax.all_to_all(stacked, axes, 0, 0, tiled=True)  63.3 us
    all_to_all x1, blocking collectives, local(): by_bin = lax.all_to_all(spectra, axes, 0, 0, tiled=True)  28.1 us
    pallas_call x1, Pallas kernels, whitened_spectra(): pl.pallas_call(whiten_kernel, in_specs=anywhere(4), out_shape=jax.ShapeDt...  10.5 us
    pallas_call x1, Pallas kernels, correlations_of(): pl.pallas_call(lag_kernel, in_specs=[*[pl.BlockSpec(memory_space=pltpu.VM...  8.9 us
    pallas_call x1, Pallas kernels, cross_spectra(): pl.pallas_call(cross_kernel, out_shape=jax.ShapeDtypeStruct((DEVICES, 2 *...  6.77 us

profile of v3, /device:TPU:1, one launch (start us, length us, event | category | flops | bytes accessed | tf_op | source)
XLA Modules:
  0.0 117.8 jit_solution(11819932487226578729)
XLA Ops:
  0.0 10.5 %whiten.1 = bf16[128,24,128]{2,1,0:T(8,128)(2,1)} custom-call(bf16[3,60,8192]{2,1,0:T(8,128)(2,1)} %x_hbm.1, s32[3,60]{1,0:T(4,128)} %m_hbm.1, bf16[4,2048,512]{2,1,0:T(8,128)(2,1)} %constant.8.clone.table_hbm, f32[8,1024]{1,0:T(8,128)} %constant.9.clone.rows_hbm), custom_call_target="tpu_custom_call" | custom-call | tf_op jit(solution)/shard_map/whiten/pallas_call | solution.py:206
  10.5 28.1 %all_to_all.10.got_ref = bf16[128,24,128]{2,1,0:T(8,128)(2,1)S(1)} all-to-all(bf16[128,24,128]{2,1,0:T(8,128)(2,1)} %whiten.1), channel_id=1, replica_groups=mesh['row'=8,'col'=16] {'row','col'}, dimensions={0} | all-to-all | bytes 1572864 | tf_op jit(solution)/shard_map/all_to_all | solution.py:382
  38.6 6.8 %cross.1 = bf16[128,16,1152]{2,1,0:T(8,128)(2,1)S(1)} custom-call(bf16[128,24,128]{2,1,0:T(8,128)(2,1)S(1)} %all_to_all.10.got_ref), custom_call_target="tpu_custom_call" | custom-call | tf_op jit(solution)/shard_map/cross/pallas_call | solution.py:284
  45.4 0.0 copy-start
  45.4 0.0 copy-start.1
  45.4 63.3 %all_to_all.11.x_ref = bf16[128,16,1152]{2,1,0:T(8,128)(2,1)S(1)} all-to-all(bf16[128,16,1152]{2,1,0:T(8,128)(2,1)S(1)} %cross.1), channel_id=1, replica_groups=mesh['row'=8,'col'=16] {'row','col'}, dimensions={0} | all-to-all | bytes 9437184 | tf_op jit(solution)/shard_map/all_to_all | solution.py:385
  108.7 0.0 copy-done
  108.7 0.0 copy-done.1
  108.7 8.9 %lags.1 = f32[16,3,24,2048]{3,2,1,0:T(8,128)} custom-call(bf16[128,16,1152]{2,1,0:T(8,128)(2,1)S(1)} %all_to_all.11.x_ref, bf16[2,2,1024,512]{3,2,1,0:T(8,128)(2,1)S(1)} %copy-done, f32[8,1024]{1,0:T(8,128)S(1)} %copy-done.1), custom_call_target="tpu_custom_call" | custom-call | tf_op jit(solution)/shard_map/lags/pallas_call | solution.py:363
Async XLA Ops:
  45.4 63.3 %copy-start = (bf16[2,2,1024,512]{3,2,1,0:T(8,128)(2,1)S(1)}, bf16[2,2,1024,512]{3,2,1,0:T(8,128)(2,1)}, u32[]{:S(2)}) copy-start(bf16[2,2,1024,512]{3,2,1,0:T(8,128)(2,1)} %constant.10.clone.table_ref) | copy-start | bytes 12582916
  45.4 63.3 %copy-start.1 = (f32[8,1024]{1,0:T(8,128)S(1)}, f32[8,1024]{1,0:T(8,128)}, u32[]{:S(2)}) copy-start(f32[8,1024]{1,0:T(8,128)} %constant.11.clone.edge_ref) | copy-start | bytes 98308

commit v4 on v3

--- a/solution.py
+++ b/solution.py
@@ -202,7 +202,12 @@
     return [pl.BlockSpec(memory_space=pl.ANY)] * count
 
 
+def in_hbm(array):
+    return pltpu.with_memory_space_constraint(array, pltpu.HBM)
+
+
 def whitened_spectra(traces, masks):
+    operands = (traces, masks, jnp.asarray(forward_tables()), jnp.asarray(window_rows()))
     return pl.pallas_call(
         whiten_kernel,
         in_specs=anywhere(4),
@@ -215,9 +220,9 @@
             pltpu.VMEM((4, 2 * OWN * SLOT, QUARTER), BF16),
             pltpu.SemaphoreType.DMA((9,)),
         ],
-        compiler_params=pltpu.CompilerParams(vmem_limit_bytes=60 * MIB),
+        compiler_params=pltpu.CompilerParams(vmem_limit_bytes=40 * MIB),
         name="whiten",
-    )(traces, masks, jnp.asarray(forward_tables()), jnp.asarray(window_rows()))
+    )(*(in_hbm(array) for array in operands))
 
 
 def cross_kernel(got_ref, out_ref, own_ref, sorted_ref, scale_ref, part_ref):
@@ -277,7 +282,7 @@
                 out_ref[g % ROWS * COLS + c, :, lanes_of] = tiles[-c % COLS]
         return carry
 
-    lax.fori_loop(0, OWN * ROWS, one_row, 0, unroll=3)
+    lax.fori_loop(0, OWN * ROWS, one_row, 0, unroll=6)
 
 
 def cross_spectra(got):
@@ -312,10 +317,10 @@
 
     copies = []
 
-    def send(i, first):
+    def send(i, first, width):
         copy = pltpu.make_async_copy(
-            out_ref.at[i, :, :, pl.ds(first, LAG_STEP)],
-            out_hbm.at[:, i, :, pl.ds(first, LAG_STEP)],
+            out_ref.at[i, :, :, pl.ds(first, width)],
+            out_hbm.at[:, i, :, pl.ds(first, width)],
             sems.at[len(copies)],
         )
         copy.start()
@@ -338,14 +343,17 @@
             even = jnp.dot(real, table_ref[n, 0], preferred_element_type=F32)
             odd = jnp.dot(imag, table_ref[n, 1], preferred_element_type=F32)
             store(i, HALF + LAG_STEP * n, even + odd)
-            send(i, HALF + LAG_STEP * n)
             back = even - odd
             for t in reversed(range(LAG_STEP // 128)):
                 turned = jnp.take_along_axis(back[:, 128 * t : 128 * (t + 1)], mirror, axis=1)
                 first = HALF - LAG_STEP * n - 128 * (t + 1)
                 store(i, first, jnp.where(lane == 0, before, turned))
                 before = turned
-            send(i, HALF - LAG_STEP * (n + 1))
+            if i == OWN - 1:
+                send(i, HALF + LAG_STEP * n, LAG_STEP)
+                send(i, HALF - LAG_STEP * (n + 1), LAG_STEP)
+        if i < OWN - 1:
+            send(i, 0, LAGS)
     for copy in copies:
         copy.wait()
 

time: 118 us -> 115 us (0.975)
  Pallas kernels: 26.2 us -> 24 us
where the time goes in v4:
time: 115 us
  blocking collectives  91.2 us (79%)
  Pallas kernels  24 us (21%)
    all_to_all x1, blocking collectives, local(): by_pair = lax.all_to_all(stacked, axes, 0, 0, tiled=True)  63.3 us
    all_to_all x1, blocking collectives, local(): by_bin = lax.all_to_all(spectra, axes, 0, 0, tiled=True)  27.9 us
    pallas_call x1, Pallas kernels, whitened_spectra(): pl.pallas_call(whiten_kernel, in_specs=anywhere(4), out_shape=jax.ShapeDt...  9.64 us
    pallas_call x1, Pallas kernels, correlations_of(): pl.pallas_call(lag_kernel, in_specs=[*[pl.BlockSpec(memory_space=pltpu.VM...  7.83 us
    pallas_call x1, Pallas kernels, cross_spectra(): pl.pallas_call(cross_kernel, out_shape=jax.ShapeDtypeStruct((DEVICES, 2 *...  6.52 us

profile of v4, /device:TPU:1, one launch (start us, length us, event | category | flops | bytes accessed | tf_op | source)
XLA Modules:
  0.0 115.4 jit_solution(13496640171997620660)
XLA Ops:
  0.0 9.6 %whiten.1 = bf16[128,24,128]{2,1,0:T(8,128)(2,1)S(1)} custom-call(bf16[3,60,8192]{2,1,0:T(8,128)(2,1)} %x_hbm.1, s32[3,60]{1,0:T(4,128)} %m_hbm.1, bf16[4,2048,512]{2,1,0:T(8,128)(2,1)} %constant.8.clone.table_hbm, f32[8,1024]{1,0:T(8,128)} %constant.9.clone.rows_hbm), custom_call_target="tpu_custom_call" | custom-call | tf_op jit(solution)/shard_map/whiten/pallas_call | solution.py:211
  9.6 27.9 %all_to_all.10.got_ref = bf16[128,24,128]{2,1,0:T(8,128)(2,1)S(1)} all-to-all(bf16[128,24,128]{2,1,0:T(8,128)(2,1)S(1)} %whiten.1), channel_id=1, replica_groups=mesh['row'=8,'col'=16] {'row','col'}, dimensions={0} | all-to-all | bytes 1572864 | tf_op jit(solution)/shard_map/all_to_all | solution.py:390
  37.5 6.5 %cross.1 = bf16[128,16,1152]{2,1,0:T(8,128)(2,1)S(1)} custom-call(bf16[128,24,128]{2,1,0:T(8,128)(2,1)S(1)} %all_to_all.10.got_ref), custom_call_target="tpu_custom_call" | custom-call | tf_op jit(solution)/shard_map/cross/pallas_call | solution.py:289
  44.0 0.0 copy-start
  44.0 0.0 copy-start.1
  44.1 63.3 %all_to_all.11.x_ref = bf16[128,16,1152]{2,1,0:T(8,128)(2,1)S(1)} all-to-all(bf16[128,16,1152]{2,1,0:T(8,128)(2,1)S(1)} %cross.1), channel_id=1, replica_groups=mesh['row'=8,'col'=16] {'row','col'}, dimensions={0} | all-to-all | bytes 9437184 | tf_op jit(solution)/shard_map/all_to_all | solution.py:393
  107.4 0.0 copy-done
  107.4 0.0 copy-done.1
  107.4 7.8 %lags.1 = f32[16,3,24,2048]{3,2,1,0:T(8,128)} custom-call(bf16[128,16,1152]{2,1,0:T(8,128)(2,1)S(1)} %all_to_all.11.x_ref, bf16[2,2,1024,512]{3,2,1,0:T(8,128)(2,1)S(1)} %copy-done, f32[8,1024]{1,0:T(8,128)S(1)} %copy-done.1), custom_call_target="tpu_custom_call" | custom-call | tf_op jit(solution)/shard_map/lags/pallas_call | solution.py:371
Async XLA Ops:
  44.0 63.3 %copy-start = (bf16[2,2,1024,512]{3,2,1,0:T(8,128)(2,1)S(1)}, bf16[2,2,1024,512]{3,2,1,0:T(8,128)(2,1)}, u32[]{:S(2)}) copy-start(bf16[2,2,1024,512]{3,2,1,0:T(8,128)(2,1)} %constant.10.clone.table_ref) | copy-start | bytes 12582916
  44.0 63.3 %copy-start.1 = (f32[8,1024]{1,0:T(8,128)S(1)}, f32[8,1024]{1,0:T(8,128)}, u32[]{:S(2)}) copy-start(f32[8,1024]{1,0:T(8,128)} %constant.11.clone.edge_ref) | copy-start | bytes 98308

commit v5 on v4

--- a/solution.py
+++ b/solution.py
@@ -114,15 +114,19 @@
     for i in range(OWN):
         part = [x_ref[i, :, QUARTER * j : QUARTER * (j + 1)].astype(F32) for j in range(4)]
         even, odd = part[0] + part[2], part[1] + part[3]
-        kinds = (even + odd, even - odd, part[0] - part[2], part[1] - part[3])
-        for kind, value in enumerate(kinds):
+        for kind, value in enumerate((even + odd, even - odd)):
             high, low = halves(value)
             u_ref[kind, SLOT * i : SLOT * i + TRACES, :] = high
             u_ref[kind, span + SLOT * i : span + SLOT * i + TRACES, :] = low
+        for j in range(4):
+            first = span * (j // 2) + SLOT * i
+            u_ref[2 + j % 2, first : first + TRACES, :] = x_ref[
+                i, :, QUARTER * j : QUARTER * (j + 1)
+            ]
 
     def times_table(kind, q):
         both = jnp.dot(u_ref[kind], table_ref[q], preferred_element_type=F32)
-        both = both[:span] + both[span:]
+        both = both[:span] + both[span:] if kind < 2 else both[:span] - both[span:]
         return both[:, :CLASS], both[:, CLASS:]
 
     reals, imags = {}, {}

time: 115 us -> 115 us (level)
  no operation moved by 1% of the time
where the time goes in v5:
time: 115 us
  blocking collectives  91.2 us (79%)
  Pallas kernels  23.6 us (21%)
    all_to_all x1, blocking collectives, local(): by_pair = lax.all_to_all(stacked, axes, 0, 0, tiled=True)  63.3 us
    all_to_all x1, blocking collectives, local(): by_bin = lax.all_to_all(spectra, axes, 0, 0, tiled=True)  27.9 us
    pallas_call x1, Pallas kernels, whitened_spectra(): pl.pallas_call(whiten_kernel, in_specs=anywhere(4), out_shape=jax.ShapeDt...  9.2 us
    pallas_call x1, Pallas kernels, correlations_of(): pl.pallas_call(lag_kernel, in_specs=[*[pl.BlockSpec(memory_space=pltpu.VM...  7.83 us
    pallas_call x1, Pallas kernels, cross_spectra(): pl.pallas_call(cross_kernel, out_shape=jax.ShapeDtypeStruct((DEVICES, 2 *...  6.52 us

profile of v5, /device:TPU:1, one launch (start us, length us, event | category | flops | bytes accessed | tf_op | source)
XLA Modules:
  0.0 114.9 jit_solution(4519528434080590599)
XLA Ops:
  0.0 9.2 %whiten.1 = bf16[128,24,128]{2,1,0:T(8,128)(2,1)S(1)} custom-call(bf16[3,60,8192]{2,1,0:T(8,128)(2,1)} %x_hbm.1, s32[3,60]{1,0:T(4,128)} %m_hbm.1, bf16[4,2048,512]{2,1,0:T(8,128)(2,1)} %constant.8.clone.table_hbm, f32[8,1024]{1,0:T(8,128)} %constant.9.clone.rows_hbm), custom_call_target="tpu_custom_call" | custom-call | tf_op jit(solution)/shard_map/whiten/pallas_call | solution.py:215
  9.2 27.9 %all_to_all.10.got_ref = bf16[128,24,128]{2,1,0:T(8,128)(2,1)S(1)} all-to-all(bf16[128,24,128]{2,1,0:T(8,128)(2,1)S(1)} %whiten.1), channel_id=1, replica_groups=mesh['row'=8,'col'=16] {'row','col'}, dimensions={0} | all-to-all | bytes 1572864 | tf_op jit(solution)/shard_map/all_to_all | solution.py:394
  37.1 6.5 %cross.1 = bf16[128,16,1152]{2,1,0:T(8,128)(2,1)S(1)} custom-call(bf16[128,24,128]{2,1,0:T(8,128)(2,1)S(1)} %all_to_all.10.got_ref), custom_call_target="tpu_custom_call" | custom-call | tf_op jit(solution)/shard_map/cross/pallas_call | solution.py:293
  43.6 0.0 copy-start
  43.6 0.0 copy-start.1
  43.6 63.3 %all_to_all.11.x_ref = bf16[128,16,1152]{2,1,0:T(8,128)(2,1)S(1)} all-to-all(bf16[128,16,1152]{2,1,0:T(8,128)(2,1)S(1)} %cross.1), channel_id=1, replica_groups=mesh['row'=8,'col'=16] {'row','col'}, dimensions={0} | all-to-all | bytes 9437184 | tf_op jit(solution)/shard_map/all_to_all | solution.py:397
  106.9 0.0 copy-done
  106.9 0.0 copy-done.1
  106.9 7.8 %lags.1 = f32[16,3,24,2048]{3,2,1,0:T(8,128)} custom-call(bf16[128,16,1152]{2,1,0:T(8,128)(2,1)S(1)} %all_to_all.11.x_ref, bf16[2,2,1024,512]{3,2,1,0:T(8,128)(2,1)S(1)} %copy-done, f32[8,1024]{1,0:T(8,128)S(1)} %copy-done.1), custom_call_target="tpu_custom_call" | custom-call | tf_op jit(solution)/shard_map/lags/pallas_call | solution.py:375
Async XLA Ops:
  43.6 63.3 %copy-start = (bf16[2,2,1024,512]{3,2,1,0:T(8,128)(2,1)S(1)}, bf16[2,2,1024,512]{3,2,1,0:T(8,128)(2,1)}, u32[]{:S(2)}) copy-start(bf16[2,2,1024,512]{3,2,1,0:T(8,128)(2,1)} %constant.10.clone.table_ref) | copy-start | bytes 12582916
  43.6 63.3 %copy-start.1 = (f32[8,1024]{1,0:T(8,128)S(1)}, f32[8,1024]{1,0:T(8,128)}, u32[]{:S(2)}) copy-start(f32[8,1024]{1,0:T(8,128)} %constant.11.clone.edge_ref) | copy-start | bytes 98308
